TPU v7x, 32 devices: a whole 2x2x4 slice. The times are simulated.
32 devices in a mesh: row: 4 (over y, core), col: 8 (over z, x).
Axes of the slice: x: 2, y: 2, z: 4, core: 2. Of those that a mesh axis runs over, the one named last changes fastest.
Arguments:
- blocks: float32 [32, 8, 256, 256], P('row', 'col'), may hold values from -6 to 6
- panel_rows: int32 [2, 16], P(None, 'row'), may hold values from -1 to 191, as said below
- target_slots: int32 [2, 32, 8], P(None, 'row', 'col'), may hold values from -1 to 3, as said below
- diag_inverse: float32 [2, 256, 256], replicated, may hold values from -1 to 1, as said below
- cross_block: float32 [256, 256], replicated, may hold values from -6 to 6
Outputs:
- factored: float32 [32, 8, 256, 256], P('row', 'col')
Inputs may be any that keep to these rules, and one draw needn't show every extreme that they name: `panel_rows`: slot q * 2 + m of row device r stands for the m-th structure row of block column class r + q times the number of row devices; both lists are -1 where that class is 0 or 1, and list 0 is -1 also where block column 0 lacks the row; otherwise list 0 equals list 1. `target_slots`: A filled slot of class c names in entry 0 a slot of its own row device and in entry 1 a slot of row device c modulo the number of row devices, within (c // number of row devices) * 2 and the 1 after it; both are filled or both -1, always -1 in classes 0 and 1; the target's block row number is at least its block column number. `diag_inverse`: each matrix is lower triangular.
All inputs are finite; a program needn't handle non-finite values.
Results may differ from a plain program's by a relative error of at most 0.0003.
Values sent between devices are 32-bit elements; how exact they have to be, the bound alone decides.
A program may use at most 128 MiB of HBM per device.

v0:
```python
import jax
import jax.numpy as jnp
from jax import lax
from jax.sharding import PartitionSpec as P

PER_CLASS = 2


HIGHEST_PRECISION = lax.Precision.HIGHEST


def broadcast(array, axis, root):
    mine = lax.axis_index(axis) == root
    return lax.psum(jnp.where(mine, array, jnp.zeros_like(array)), axis)


def apply_inverse(panel_blocks, inverse):
    return jnp.einsum("sab,cb->sac", panel_blocks, inverse, precision=HIGHEST_PRECISION)


def per_device(blocks, panel_rows, target_slots, diag_inverse, cross_block):
    column = lax.axis_index("col")
    row_count = lax.axis_size("row")
    stored = blocks[:, 0]
    slot_count = panel_rows.shape[1]
    head_part = stored[:slot_count]
    first_live = (panel_rows[0] >= 0)[:, None, None]
    second_live = (panel_rows[1] >= 0)[:, None, None]
    cross_factor = jnp.dot(cross_block, diag_inverse[0].T, precision=HIGHEST_PRECISION)
    blank_part = jnp.zeros_like(head_part)
    class_start = column // row_count * PER_CLASS
    owner_row = column % row_count
    first_factor = lax.cond(
        column == 0,
        lambda: jnp.where(first_live, apply_inverse(head_part, diag_inverse[0]), 0.0),
        lambda: blank_part,
    )
    first_rows = broadcast(first_factor, "col", 0)
    first_cols = broadcast(
        lax.dynamic_slice_in_dim(first_rows, class_start, PER_CLASS, 0), "row", owner_row
    )
    second_factor = lax.cond(
        column == 1,
        lambda: jnp.where(
            second_live,
            apply_inverse(head_part - apply_inverse(first_rows, cross_factor), diag_inverse[1]),
            0.0,
        ),
        lambda: blank_part,
    )
    second_rows = broadcast(second_factor, "col", 1)
    second_cols = broadcast(
        lax.dynamic_slice_in_dim(second_rows, class_start, PER_CLASS, 0), "row", owner_row
    )
    row_index = target_slots[0, :, 0]
    col_index = target_slots[1, :, 0]
    present = row_index >= 0
    left_slot = jnp.where(present, row_index, 0)
    right_slot = jnp.where(present, col_index - class_start, 0)
    left_blocks = jnp.concatenate([first_rows[left_slot], second_rows[left_slot]], axis=2)
    right_blocks = jnp.concatenate([first_cols[right_slot], second_cols[right_slot]], axis=2)
    schur_term = jnp.einsum("sak,sbk->sab", left_blocks, right_blocks, precision=HIGHEST_PRECISION)
    trailing = stored - jnp.where(present[:, None, None], schur_term, 0.0)
    own_panel = jnp.where(column == 0, first_factor, second_factor)
    keep_mask = (column == 0) & first_live | (column == 1) & second_live
    head_blocks = jnp.where(keep_mask, own_panel, trailing[:slot_count])
    factored = jnp.concatenate([head_blocks, trailing[slot_count:]], axis=0)
    return factored[:, None]


def solution(mesh):
    return jax.shard_map(
        per_device,
        mesh=mesh,
        in_specs=(P("row", "col", None, None), P(None, "row"), P(None, "row", "col"), P(), P()),
        out_specs=P("row", "col", None, None),
        check_vma=False,
    )
```

profile of v0, /device:TPU:25, one launch (start us, length us, event | category | flops | bytes accessed | tf_op | source)
XLA Modules:
  0.0 230.9 jit_solution(7812680136265645549)
XLA Ops:
  6.5 0.0 copy-start
  6.5 0.0 all-reduce.5.cloned.1.call-start
  6.6 1.4 slice_bitcast_fusion
  7.9 0.0 copy-done.4
  8.0 0.0 copy-done.3
  8.0 0.1 conditional.2
  8.0 0.1 broadcast.123
  8.1 1.1 broadcast_select_fusion.1
  9.2 0.0 all-reduce.5.cloned.1.call-update
  9.2 0.0 all-reduce.7.cloned.1.call-start
  9.2 0.0 copy-done
  9.3 0.4 fusion.16
  9.7 77.7 %all-reduce.5.cloned.1.call-done = f32[4,256,256]{2,1,0:T(8,128)} async-done(((f32[4,256,256]{2,1,0:T(8,128)}), f32[4,256,256]{2,1,0:T(8,128)}) %all-reduce.5.cloned.1.call-update) | async-done | bytes 1048592 | tf_op jit(solution)/shard_map/psum | solution.py:14
  87.4 0.1 conditional.3
  87.4 0.1 broadcast.124
  87.5 0.0 copy-start.1
  87.5 1.1 broadcast_select_fusion
  88.6 0.0 all-reduce.7.cloned.1.call-update
  88.6 0.0 all-reduce.9.cloned.1.call-start
  88.7 0.4 copy-done.1
  89.1 0.8 dynamic-slice_select_fusion.1
  89.9 79.0 %all-reduce.7.cloned.1.call-done = f32[4,256,256]{2,1,0:T(8,128)} async-done(((f32[4,256,256]{2,1,0:T(8,128)}), f32[4,256,256]{2,1,0:T(8,128)}) %all-reduce.7.cloned.1.call-update) | async-done | bytes 1048592 | tf_op jit(solution)/shard_map/psum | solution.py:14
  168.9 1.9 dynamic-slice_select_fusion
  170.8 0.0 all-reduce.9.cloned.1.call-update
  170.9 2.0 gather_fusion
  172.9 3.2 %gather_fusion.1 = f32[8,256,256]{2,1,0:T(8,128)} fusion(f32[4,256,256]{2,1,0:T(8,128)} %all-reduce.7.cloned.1.call-done, s32[1024]{0:T(1024)S(1)} %get-tuple-element.51), kind=kCustom, calls=%fused_computation.1 | custom fusion | bytes 4194336 | tf_op jit(solution)/shard_map/gather | solution.py:60
  176.1 33.2 %all-reduce.9.cloned.1.call-done = (f32[2,256,256]{2,1,0:T(8,128)}, f32[2,256,256]{2,1,0:T(8,128)}) async-done(((f32[2,256,256]{2,1,0:T(8,128)}, f32[2,256,256]{2,1,0:T(8,128)}), (f32[2,256,256]{2,1,0:T(8,128)}, f32[2,256,256]{2,1,0:T(8,128)})) %all-reduce.9.cloned.1.call-update) | async-done | bytes 1048592 | tf_op jit(solution)/shard_map/psum | solution.py:14
  209.3 3.1 %gather_fusion.3 = f32[8,256,256]{2,1,0:T(8,128)} fusion(f32[2,256,256]{2,1,0:T(8,128)} %get-tuple-element.42, s32[1024]{0:T(1024)S(1)} %get-tuple-element.50), kind=kCustom, calls=%fused_computation.3 | custom fusion | bytes 4194336 | tf_op jit(solution)/shard_map/gather | solution.py:61
  212.4 2.0 gather_fusion.2
  214.5 8.1 %bitcast_subtract_fusion = f32[8,256,256]{2,1,0:T(8,128)S(1)} fusion(f32[8,1,256,256]{3,2,1,0:T(8,128)} %param.9, pred[8]{0:T(512)(128)(4,1)S(1)} %compare_bitcast_fusion.1, f32[8,256,256]{2,1,0:T(8,128)} %gather_fusion.3, f32[8,256,256]{2,1,0:T(8,128)} %gather_fusion.2, f32[8,256,256]{2,1,0:T(8,128)} %gather_fusion.1, f32[8,256,256]{2,1,0:T(8,128)} %gather_fusion), kind=kOutput, calls=%fused_computation.21 | convolution fusion | flops 3224371200 | bytes 12582920 | tf_op jit(solution)/shard_map/sak,sbk->sab/dot_general | solution.py:62
  222.5 0.3 slice_select_fusion
  222.9 1.6 maximum_bitcast_fusion
  (11 shorter events, 0.0 us)
Async XLA Ops:
  6.5 2.7 %copy-start = (f32[256,256]{1,0:T(8,128)S(1)}, f32[256,256]{1,0:T(8,128)}, u32[]{:S(2)}) copy-start(f32[256,256]{1,0:T(8,128)} %param.13) | copy-start | bytes 786436
  6.5 1.4 copy-start.4
  6.5 1.4 copy-start.3
  6.5 80.8 %all-reduce.5.cloned.1.call-start = ((), (), s32[]{:S(2)}) async-start(), calls=%async_computation | async-start | bytes 2097152 | tf_op jit(solution)/shard_map/psum | solution.py:14
  9.2 159.7 %all-reduce.7.cloned.1.call-start = ((), (), s32[]{:S(2)}) async-start(), calls=%async_computation.1 | async-start | bytes 2097152 | tf_op jit(solution)/shard_map/psum | solution.py:14
  87.5 1.6 copy-start.1
  88.6 82.3 %copy-start.5 = (s32[2,8,1]{1,2,0:T(1,128)S(1)}, s32[2,8,1]{1,2,0:T(1,128)}, u32[]{:S(2)}) copy-start(s32[2,8,1]{1,2,0:T(1,128)} %param.11) | copy-start | bytes 196
  88.6 120.8 %all-reduce.9.cloned.1.call-start = ((), (), s32[]{:S(2)}) async-start(), calls=%async_computation.2 | async-start | bytes 2097152 | tf_op jit(solution)/shard_map/psum | solution.py:14
  209.3 3.1 %copy-start.2 = (f32[2,256,256]{2,1,0:T(8,128)S(1)}, f32[2,256,256]{2,1,0:T(8,128)}, u32[]{:S(2)}) copy-start(f32[2,256,256]{2,1,0:T(8,128)} %get-tuple-element.43) | copy-start | bytes 1572868
Sparse Core Ops, SparseCore 0:
  10.9 76.4 all-reduce.4
  91.3 77.5 all-reduce.6
  171.4 37.9 all-reduce.8
where the time goes:
time: 233 us; the launch traced here: 231 us
  waiting for transfers between devices  190 us (82%)
  between operations  13.3 us (6%)
  local copies, waits for them, and re-layouts  12.3 us (5%)
  matrix products  8.46 us (4%)
  other arithmetic  6.73 us (3%)
    psum x3, waiting for transfers between devices, broadcast(): return lax.psum(jnp.where(mine, array, jnp.zeros_like(array)), axis)  190 us
    dot_general x1, matrix products, per_device(): jnp.einsum('sak,sbk->sab', left_blocks, right_blocks, precision=HIGHEST_P...  8.05 us
    select_n x4, other arithmetic, broadcast(): return lax.psum(jnp.where(mine, array, jnp.zeros_like(array)), axis)  4.85 us
  transfers between devices with their start and end apart: 3, of which 3 were waited for; matrix products, arithmetic and copies ran while one was open for 3% of the time, Pallas kernels for 0%

commit v1 on v0

v1 whole, which is shorter than its diff:
```python
import functools

import jax
import jax.numpy as jnp
from jax import lax
from jax.experimental import pallas as pl
from jax.experimental.pallas import tpu as pltpu
from jax.sharding import PartitionSpec as P

PER_CLASS = 2
CHUNK = 64
MESH = pl.DeviceIdType.MESH
F32 = jnp.float32
BF16 = jnp.bfloat16
NN = (((1,), (0,)), ((), ()))
NT = (((1,), (1,)), ((), ()))


def split(x):
    high = x.astype(BF16)
    return high, (x - high.astype(F32)).astype(BF16)


def product(a, b, dims=NN):
    (ah, al), (bh, bl) = a, b
    dot = functools.partial(lax.dot_general, dimension_numbers=dims, preferred_element_type=F32)
    return dot(ah, bh) + (dot(ah, bl) + dot(al, bh))


def kernel(
    n_row, n_col, n_x,
    blocks, panel_rows, target_slots, diag_inverse, cross_block, out,
    own, left, right, terms, mixed_high, mixed_low,
    own_sem, left_recv, left_send, right_recv, right_send,
):
    n_y, n_z = n_row // 2, n_col // n_x
    slots, _, size, _ = blocks.shape
    panel = panel_rows.shape[1]
    pieces = size // CHUNK
    row, col = lax.axis_index("row"), lax.axis_index("col")
    y, core = lax.div(row, 2), lax.rem(row, 2)
    z, x = lax.div(col, n_x), lax.rem(col, n_x)

    def at(yy, cc, zz, xx):
        return (yy * 2 + cc, zz * n_x + xx)

    owner = lax.rem(col, n_row)
    owner_y, owner_core = lax.div(owner, 2), lax.rem(owner, 2)
    class_start = lax.div(col, n_row) * PER_CLASS
    has_targets = col >= 2
    holder = row == owner
    first_piece = jnp.where(row < 2, PER_CLASS * pieces, 0)

    for slot in range(slots):
        pltpu.make_async_copy(blocks.at[slot, 0], own.at[slot], own_sem.at[slot]).start()

    neighbours = (
        (z > 0, at(y, core, z - 1, x)),
        (z < n_z - 1, at(y, core, z + 1, x)),
        (x > 0, at(y, core, z, x - 1)),
        (x < n_x - 1, at(y, core, z, x + 1)),
        (y > 0, at(y - 1, core, z, x)),
        (y < n_y - 1, at(y + 1, core, z, x)),
        (row >= 0, at(y, 1 - core, z, x)),
    )
    barrier = pltpu.get_barrier_semaphore()
    expected = 0
    for exists, device in neighbours:
        @pl.when(exists)
        def _():
            pl.semaphore_signal(barrier, inc=1, device_id=device, device_id_type=MESH)
        expected = expected + jnp.where(exists, 1, 0)
    pl.semaphore_wait(barrier, expected)

    for slot in range(slots):
        pltpu.make_async_copy(blocks.at[slot, 0], own.at[slot], own_sem.at[slot]).wait()
    for stream in range(2):
        @pl.when(col == stream)
        def _():
            for slot in range(panel):
                live = jnp.full((size, size), panel_rows[stream, slot], jnp.int32) >= 0
                left[stream, slot] = jnp.where(live, own[slot], 0.0)

    def left_piece(stream, piece):
        rows = pl.ds(pl.multiple_of(lax.rem(piece, pieces) * CHUNK, CHUNK), CHUNK)
        return left.at[stream, lax.div(piece, pieces), rows]

    def right_piece(stream, piece):
        rows = pl.ds(pl.multiple_of(lax.rem(piece, pieces) * CHUNK, CHUNK), CHUNK)
        return right.at[stream, lax.div(piece, pieces), rows]

    def left_hops(stream):
        along_z = (x == stream) & (z < n_z - 1)
        up = (x >= stream) & (x < n_x - 1)
        down = (x <= stream) & (x > 0) & ((z > 0) | (x > 1))
        return (
            (along_z, at(y, core, z + 1, x)),
            (up, at(y, core, z, x + 1)),
            (down, at(y, core, z, x - 1)),
        )

    gets = (col != 0, (col != 0) & (col != 1))

    right_hops = (
        (has_targets & (core == owner_core) & (y >= owner_y) & (y < n_y - 1), at(y + 1, core, z, x)),
        (has_targets & (core == owner_core) & (y <= owner_y) & (y > 0), at(y - 1, core, z, x)),
        (has_targets & (core == owner_core), at(y, 1 - core, z, x)),
    )

    def left_copy(stream, hop, device, piece):
        part = left_piece(stream, piece)
        return pltpu.make_async_remote_copy(
            src_ref=part, dst_ref=part,
            send_sem=left_send.at[hop, stream, piece], recv_sem=left_recv.at[stream, piece],
            device_id=device, device_id_type=MESH,
        )

    def right_copy(source, stream, hop, device, piece):
        return pltpu.make_async_remote_copy(
            src_ref=source, dst_ref=right_piece(stream, piece),
            send_sem=right_send.at[hop, stream, piece], recv_sem=right_recv.at[stream, piece],
            device_id=device, device_id_type=MESH,
        )

    def left_step(piece, carry):
        for stream in range(2):
            @pl.when(gets[stream])
            def _():
                left_copy(stream, 0, (row, col), piece).wait_recv()
            for hop, (wanted, device) in enumerate(left_hops(stream)):
                @pl.when(wanted)
                def _():
                    left_copy(stream, hop, device, piece).start()

        owned = piece - class_start * pieces
        @pl.when(has_targets & holder & (owned >= 0) & (owned < PER_CLASS * pieces))
        def _():
            for stream in range(2):
                for hop, (wanted, device) in enumerate(right_hops):
                    @pl.when(wanted)
                    def _():
                        right_copy(left_piece(stream, piece), stream, hop, device, owned).start()

        arriving = piece - (panel - PER_CLASS) * pieces
        @pl.when(has_targets & jnp.logical_not(holder) & (arriving >= 0))
        def _():
            for stream in range(2):
                part = right_piece(stream, arriving)
                right_copy(part, stream, 0, (row, col), arriving).wait_recv()
                for hop, (wanted, device) in enumerate(right_hops):
                    @pl.when(wanted)
                    def _():
                        right_copy(part, stream, hop, device, arriving).start()
        return carry

    lax.fori_loop(first_piece, panel * pieces, left_step, 0)

    inverse0, inverse1 = split(diag_inverse[0]), split(diag_inverse[1])
    cross = product(split(cross_block[...]), inverse0, NT)
    cross_parts = split(cross)

    @pl.when(col == 0)
    def _():
        for slot in range(panel):
            live = jnp.full((size, size), panel_rows[0, slot], jnp.int32) >= 0
            first = product(split(left[0, slot]), inverse0, NT)
            out[slot, 0] = jnp.where(live, first, own[slot])
        for slot in range(panel, slots):
            out[slot, 0] = own[slot]

    @pl.when(col == 1)
    def _():
        for slot in range(panel):
            live = jnp.full((size, size), panel_rows[1, slot], jnp.int32) >= 0
            body = own[slot]

            def second_of():
                first = product(split(left[0, slot]), inverse0, NT)
                updated = body - product(split(first), cross_parts, NT)
                return product(split(updated), inverse1, NT)

            if slot < PER_CLASS:
                @pl.when(row < 2)
                def _():
                    out[slot, 0] = body

                @pl.when(row >= 2)
                def _():
                    out[slot, 0] = jnp.where(live, second_of(), body)
            else:
                out[slot, 0] = jnp.where(live, second_of(), body)
        for slot in range(panel, slots):
            out[slot, 0] = own[slot]

    @pl.when(has_targets)
    def _():
        @pl.when(holder)
        def _():
            for stream in range(2):
                for m in range(PER_CLASS):
                    right[stream, m] = left[stream, class_start + m]

        inverse0_t, inverse1_t = split(diag_inverse[0].T), split(diag_inverse[1].T)
        cross_t = split(cross.T)
        wide = PER_CLASS * size
        first_t = product(inverse0, split(right[0].reshape(wide, size)), NT)
        second_t = product(inverse1, split(right[1].reshape(wide, size)), NT) - product(
            inverse1, split(product(cross_parts, split(first_t)))
        )
        upper = product(inverse1_t, split(second_t))
        lower = product(inverse0_t, split(first_t - product(cross_t, split(upper))))
        for place, part in ((0, lower), (size, upper)):
            high, low = split(part)
            mixed_high[place:place + size, :] = high
            mixed_low[place:place + size, :] = low

        def slot_step(slot, carry):
            both = jnp.concatenate([left[0, slot], left[1, slot]], axis=1)
            term = product(split(both), (mixed_high[...], mixed_low[...]))
            for m in range(PER_CLASS):
                terms[slot * PER_CLASS + m] = term[:, m * size:(m + 1) * size]
            return carry

        lax.fori_loop(lax.div(first_piece, pieces), panel, slot_step, 0)

        @pl.when(row < 2)
        def _():
            for slot in range(PER_CLASS * PER_CLASS):
                terms[slot] = jnp.zeros((size, size), F32)

        for slot in range(slots):
            row_index = target_slots[0, slot, 0]
            col_index = target_slots[1, slot, 0]
            place = jnp.where(
                row_index >= 0,
                row_index * PER_CLASS + jnp.clip(col_index - class_start, 0, PER_CLASS - 1),
                0,
            )
            present = jnp.full((size, size), row_index, jnp.int32) >= 0
            out[slot, 0] = own[slot] - jnp.where(present, terms[place], 0.0)

    def drain(piece, carry):
        for stream in range(2):
            for hop, (wanted, device) in enumerate(left_hops(stream)):
                @pl.when(wanted)
                def _():
                    left_copy(stream, hop, device, piece).wait_send()
        return carry

    lax.fori_loop(first_piece, panel * pieces, drain, 0)

    def drain_right(piece, carry):
        for stream in range(2):
            for hop, (wanted, device) in enumerate(right_hops):
                @pl.when(wanted)
                def _():
                    part = right_piece(stream, piece)
                    right_copy(part, stream, hop, device, piece).wait_send()
        return carry

    lax.fori_loop(0, PER_CLASS * pieces, drain_right, 0)


def per_device(n_row, n_col, n_x, blocks, panel_rows, target_slots, diag_inverse, cross_block):
    slots, _, size, _ = blocks.shape
    panel = panel_rows.shape[1]
    count = panel * (size // CHUNK)
    right_count = PER_CLASS * (size // CHUNK)
    vmem = pl.BlockSpec(memory_space=pltpu.VMEM)
    smem = pl.BlockSpec(memory_space=pltpu.SMEM)
    return pl.pallas_call(
        functools.partial(kernel, n_row, n_col, n_x),
        out_shape=jax.ShapeDtypeStruct(blocks.shape, blocks.dtype),
        in_specs=[pl.BlockSpec(memory_space=pl.ANY), smem, smem, vmem, vmem],
        out_specs=vmem,
        scratch_shapes=[
            pltpu.VMEM((slots, size, size), F32),
            pltpu.VMEM((2, panel, size, size), F32),
            pltpu.VMEM((2, PER_CLASS, size, size), F32),
            pltpu.VMEM((panel * PER_CLASS, size, size), F32),
            pltpu.VMEM((2 * size, PER_CLASS * size), BF16),
            pltpu.VMEM((2 * size, PER_CLASS * size), BF16),
            pltpu.SemaphoreType.DMA((slots,)),
            pltpu.SemaphoreType.DMA((2, count)),
            pltpu.SemaphoreType.DMA((3, 2, count)),
            pltpu.SemaphoreType.DMA((2, right_count)),
            pltpu.SemaphoreType.DMA((3, 2, right_count)),
        ],
        compiler_params=pltpu.CompilerParams(
            collective_id=0, has_side_effects=True, vmem_limit_bytes=48 * 2**20
        ),
        cost_estimate=pl.CostEstimate(
            flops=2 * size**3 * 34 * 3, bytes_accessed=8 * slots * size * size, transcendentals=0
        ),
    )(blocks, panel_rows, target_slots, diag_inverse, cross_block)


def solution(mesh):
    n_row, n_col = mesh.shape["row"], mesh.shape["col"]
    n_x = n_row // 2
    return jax.shard_map(
        functools.partial(per_device, n_row, n_col, n_x),
        mesh=mesh,
        in_specs=(P("row", "col", None, None), P(None, "row"), P(None, "row", "col"), P(), P()),
        out_specs=P("row", "col", None, None),
        check_vma=False,
    )
```

time: 233 us -> 141 us (0.61)
  waiting for transfers between devices: 190 us -> 0 us
  Pallas kernels: 0 us -> 134 us
  between operations: 13.3 us -> 0.01 us
  matrix products: 8.46 us -> 0 us
  other arithmetic: 6.73 us -> 0 us
  local copies, waits for them, and re-layouts: 12.3 us -> 6.34 us
    psum x3 -> x0, waiting for transfers between devices: 190 us -> none  [broadcast(): return lax.psum(jnp.where(mine, array, jnp.zeros_like(array)), axis)]
    pallas_call x0 -> x1, Pallas kernels: none -> 134 us  [per_device(): pl.pallas_call(functools.partial(kernel, n_row, n_col, n_x), out_shape=ja...]
    gather x4 -> x0, local copies, waits for them, and re-layouts: 10.4 us -> none  [the longest x1 3.23 us: per_device(): second_rows[left_slot]]
    dot_general x2 -> x0, matrix products: 8.46 us -> none  [the longest x1 8.05 us: per_device(): jnp.einsum('sak,sbk->sab', left_blocks, right_blocks, precision=HIGHEST_P...]
    unnamed x12 -> x10, local copies, waits for them, and re-layouts: 0.44 us -> 6.34 us
    select_n x6 -> x0, other arithmetic: 5.15 us -> none  [the longest x4 4.85 us: broadcast(): return lax.psum(jnp.where(mine, array, jnp.zeros_like(array)), axis)]
  transfers between devices with their start and end apart: 3 -> 0, of which waited for: 3 -> 0; matrix products, arithmetic and copies ran while one was open for 3% -> 0% of each run, Pallas kernels for 0% -> 0%
where the time goes in v1:
time: 141 us; the launch traced here: 140 us
  Pallas kernels  134 us (95%)
  local copies, waits for them, and re-layouts  6.34 us (4%)
    pallas_call x1, Pallas kernels, per_device(): pl.pallas_call(functools.partial(kernel, n_row, n_col, n_x), out_shape=ja...  134 us
    unnamed x10, local copies, waits for them, and re-layouts  6.34 us

profile of v1, /device:TPU:25, one launch (start us, length us, event | category | flops | bytes accessed | tf_op | source)
XLA Modules:
  0.0 140.4 jit_solution(2343195810847359385)
XLA Ops:
  0.0 0.8 copy.6.target_slots
  0.8 0.0 copy-start
  0.8 1.6 %copy-done = f32[8,1,256,256]{3,2,1,0:T(8,128)S(1)} copy-done((f32[8,1,256,256]{3,2,1,0:T(8,128)S(1)}, f32[8,1,256,256]{3,2,1,0:T(8,128)}, u32[]{:S(2)}) %copy-start) | copy-done | bytes 2097176
  2.4 0.0 copy-start.1
  2.4 1.0 copy-done.1
  3.4 0.0 copy-start.2
  3.4 0.9 copy-done.2
  4.3 0.0 copy-start.3
  4.3 0.7 copy-done.3
  5.0 134.0 %shard_map.55 = f32[8,1,256,256]{3,2,1,0:T(8,128)S(1)} custom-call(f32[8,1,256,256]{3,2,1,0:T(8,128)S(1)} %copy-done, s32[2,4]{1,0:T(2,128)S(1)} %copy-done.3, s32[2,8,1]{2,1,0:T(8,128)S(1)} %copy.6.target_slots, f32[2,256,256]{2,1,0:T(8,128)S(1)} %copy-done.1, f32[256,256]{1,0:T(8,128)S(1)} %copy-done.2), custom_call_target="tpu_custom_call" | custom-call | flops 3422552064 | bytes 4194304 | tf_op jit(solution)/shard_map/pallas_call | solution.py:271
  139.1 1.3 copy.8
Async XLA Ops:
  0.8 1.6 %copy-start = (f32[8,1,256,256]{3,2,1,0:T(8,128)S(1)}, f32[8,1,256,256]{3,2,1,0:T(8,128)}, u32[]{:S(2)}) copy-start(f32[8,1,256,256]{3,2,1,0:T(8,128)} %blocks.1) | copy-start | bytes 6291460
  2.4 1.0 copy-start.1
  3.4 0.9 copy-start.2
  4.3 0.7 copy-start.3

commit v2 on v1

--- a/solution.py
+++ b/solution.py
@@ -29,9 +29,9 @@
 
 def kernel(
     n_row, n_col, n_x,
-    blocks, panel_rows, target_slots, diag_inverse, cross_block, out,
-    own, left, right, terms, mixed_high, mixed_low,
-    own_sem, left_recv, left_send, right_recv, right_send,
+    blocks, panel_rows, target_slots, inverse_in, cross_in, out,
+    diag_inverse, cross_block, own, left, right, terms, mixed_high, mixed_low,
+    given_sem, own_sem, left_recv, left_send, right_recv, right_send,
 ):
     n_y, n_z = n_row // 2, n_col // n_x
     slots, _, size, _ = blocks.shape
@@ -54,6 +54,13 @@
     for slot in range(slots):
         pltpu.make_async_copy(blocks.at[slot, 0], own.at[slot], own_sem.at[slot]).start()
 
+    given = (
+        pltpu.make_async_copy(inverse_in, diag_inverse, given_sem.at[0]),
+        pltpu.make_async_copy(cross_in, cross_block, given_sem.at[1]),
+    )
+    for copy in given:
+        copy.start()
+
     neighbours = (
         (z > 0, at(y, core, z - 1, x)),
         (z < n_z - 1, at(y, core, z + 1, x)),
@@ -61,7 +68,8 @@
         (x < n_x - 1, at(y, core, z, x + 1)),
         (y > 0, at(y - 1, core, z, x)),
         (y < n_y - 1, at(y + 1, core, z, x)),
-        (row >= 0, at(y, 1 - core, z, x)),
+        (y > 0, at(y - 1, 1 - core, z, x)),
+        (y < n_y - 1, at(y + 1, 1 - core, z, x)),
     )
     barrier = pltpu.get_barrier_semaphore()
     expected = 0
@@ -101,10 +109,16 @@
 
     gets = (col != 0, (col != 0) & (col != 1))
 
+    same, before, after = core == owner_core, y < owner_y, y > owner_y
+    up = (same & jnp.logical_not(before)) | (jnp.logical_not(same) & after)
+    up = up | (jnp.logical_not(same) & (y == owner_y - 1) & (owner_y == n_y - 1))
+    down = (same & jnp.logical_not(after)) | (jnp.logical_not(same) & before)
+    down = down | (jnp.logical_not(same) & (y == owner_y + 1))
     right_hops = (
-        (has_targets & (core == owner_core) & (y >= owner_y) & (y < n_y - 1), at(y + 1, core, z, x)),
-        (has_targets & (core == owner_core) & (y <= owner_y) & (y > 0), at(y - 1, core, z, x)),
-        (has_targets & (core == owner_core), at(y, 1 - core, z, x)),
+        (has_targets & up & (y < n_y - 1), at(y + 1, core, z, x)),
+        (has_targets & down & (y > 0), at(y - 1, core, z, x)),
+        (has_targets & holder & (y < n_y - 1), at(y + 1, 1 - core, z, x)),
+        (has_targets & holder & (y > 0), at(y - 1, 1 - core, z, x)),
     )
 
     def left_copy(stream, hop, device, piece):
@@ -122,7 +136,7 @@
             device_id=device, device_id_type=MESH,
         )
 
-    def left_step(piece, carry):
+    def left_step(piece):
         for stream in range(2):
             @pl.when(gets[stream])
             def _():
@@ -141,20 +155,31 @@
                     def _():
                         right_copy(left_piece(stream, piece), stream, hop, device, owned).start()
 
-        arriving = piece - (panel - PER_CLASS) * pieces
-        @pl.when(has_targets & jnp.logical_not(holder) & (arriving >= 0))
-        def _():
-            for stream in range(2):
-                part = right_piece(stream, arriving)
-                right_copy(part, stream, 0, (row, col), arriving).wait_recv()
-                for hop, (wanted, device) in enumerate(right_hops):
-                    @pl.when(wanted)
-                    def _():
-                        right_copy(part, stream, hop, device, arriving).start()
+    def right_step(arriving):
+        for stream in range(2):
+            part = right_piece(stream, arriving)
+            right_copy(part, stream, 0, (row, col), arriving).wait_recv()
+            for hop, (wanted, device) in enumerate(right_hops[:2]):
+                @pl.when(wanted)
+                def _():
+                    right_copy(part, stream, hop, device, arriving).start()
+
+    right_start = jnp.where(row < 2, panel * pieces, (panel - PER_CLASS) * pieces)
+
+    def step(piece, carry):
+        @pl.when(piece < panel * pieces)
+        def _():
+            left_step(piece)
+
+        @pl.when(has_targets & jnp.logical_not(holder) & (piece >= right_start))
+        def _():
+            right_step(piece - right_start)
         return carry
 
-    lax.fori_loop(first_piece, panel * pieces, left_step, 0)
-
+    lax.fori_loop(first_piece, right_start + PER_CLASS * pieces, step, 0)
+
+    for copy in given:
+        copy.wait()
     inverse0, inverse1 = split(diag_inverse[0]), split(diag_inverse[1])
     cross = product(split(cross_block[...]), inverse0, NT)
     cross_parts = split(cross)
@@ -267,24 +292,28 @@
     count = panel * (size // CHUNK)
     right_count = PER_CLASS * (size // CHUNK)
     vmem = pl.BlockSpec(memory_space=pltpu.VMEM)
+    anywhere = pl.BlockSpec(memory_space=pl.ANY)
     smem = pl.BlockSpec(memory_space=pltpu.SMEM)
     return pl.pallas_call(
         functools.partial(kernel, n_row, n_col, n_x),
         out_shape=jax.ShapeDtypeStruct(blocks.shape, blocks.dtype),
-        in_specs=[pl.BlockSpec(memory_space=pl.ANY), smem, smem, vmem, vmem],
+        in_specs=[anywhere, smem, smem, anywhere, anywhere],
         out_specs=vmem,
         scratch_shapes=[
+            pltpu.VMEM(diag_inverse.shape, F32),
+            pltpu.VMEM(cross_block.shape, F32),
             pltpu.VMEM((slots, size, size), F32),
             pltpu.VMEM((2, panel, size, size), F32),
             pltpu.VMEM((2, PER_CLASS, size, size), F32),
             pltpu.VMEM((panel * PER_CLASS, size, size), F32),
             pltpu.VMEM((2 * size, PER_CLASS * size), BF16),
             pltpu.VMEM((2 * size, PER_CLASS * size), BF16),
+            pltpu.SemaphoreType.DMA((2,)),
             pltpu.SemaphoreType.DMA((slots,)),
             pltpu.SemaphoreType.DMA((2, count)),
             pltpu.SemaphoreType.DMA((3, 2, count)),
             pltpu.SemaphoreType.DMA((2, right_count)),
-            pltpu.SemaphoreType.DMA((3, 2, right_count)),
+            pltpu.SemaphoreType.DMA((4, 2, right_count)),
         ],
         compiler_params=pltpu.CompilerParams(
             collective_id=0, has_side_effects=True, vmem_limit_bytes=48 * 2**20

time: 141 us -> 169 us (1.20)
  the two profiles are of different devices: /device:TPU:25 before, /device:TPU:30 now
where the time goes in v2:
time: 169 us
  Pallas kernels  162 us (96%)
  local copies, waits for them, and re-layouts  6.34 us (4%)
    pallas_call x1, Pallas kernels, per_device(): pl.pallas_call(functools.partial(kernel, n_row, n_col, n_x), out_shape=ja...  162 us
    unnamed x10, local copies, waits for them, and re-layouts  6.34 us

profile of v2, /device:TPU:30, one launch (start us, length us, event | category | flops | bytes accessed | tf_op | source)
XLA Modules:
  0.0 168.7 jit_solution(9523270180313249830)
XLA Ops:
  0.0 0.8 copy.6.target_slots
  0.8 0.0 copy-start
  0.8 1.6 copy-done
  2.4 0.0 copy-start.1
  2.4 1.0 copy-done.1
  3.4 0.0 copy-start.2
  3.4 0.9 copy-done.2
  4.3 0.0 copy-start.3
  4.3 0.7 copy-done.3
  5.0 162.3 %shard_map.55 = f32[8,1,256,256]{3,2,1,0:T(8,128)S(1)} custom-call(f32[8,1,256,256]{3,2,1,0:T(8,128)S(1)} %copy-done, s32[2,4]{1,0:T(2,128)S(1)} %copy-done.3, s32[2,8,1]{2,1,0:T(8,128)S(1)} %copy.6.target_slots, f32[2,256,256]{2,1,0:T(8,128)S(1)} %copy-done.1, f32[256,256]{1,0:T(8,128)S(1)} %copy-done.2), custom_call_target="tpu_custom_call" | custom-call | flops 3422552064 | bytes 4194304 | tf_op jit(solution)/shard_map/pallas_call | solution.py:297
  167.4 1.3 copy.8
Async XLA Ops:
  0.8 1.6 copy-start
  2.4 1.0 copy-start.1
  3.4 0.9 copy-start.2
  4.3 0.7 copy-start.3

commit v3 on v2

--- a/solution.py
+++ b/solution.py
@@ -9,6 +9,7 @@
 
 PER_CLASS = 2
 CHUNK = 64
+LAG = 3
 MESH = pl.DeviceIdType.MESH
 F32 = jnp.float32
 BF16 = jnp.bfloat16
@@ -136,24 +137,22 @@
             device_id=device, device_id_type=MESH,
         )
 
-    def left_step(piece):
-        for stream in range(2):
-            @pl.when(gets[stream])
+    def left_step(stream, piece):
+        @pl.when(gets[stream])
+        def _():
+            left_copy(stream, 0, (row, col), piece).wait_recv()
+        for hop, (wanted, device) in enumerate(left_hops(stream)):
+            @pl.when(wanted)
             def _():
-                left_copy(stream, 0, (row, col), piece).wait_recv()
-            for hop, (wanted, device) in enumerate(left_hops(stream)):
-                @pl.when(wanted)
-                def _():
-                    left_copy(stream, hop, device, piece).start()
+                left_copy(stream, hop, device, piece).start()
 
         owned = piece - class_start * pieces
         @pl.when(has_targets & holder & (owned >= 0) & (owned < PER_CLASS * pieces))
         def _():
-            for stream in range(2):
-                for hop, (wanted, device) in enumerate(right_hops):
-                    @pl.when(wanted)
-                    def _():
-                        right_copy(left_piece(stream, piece), stream, hop, device, owned).start()
+            for hop, (wanted, device) in enumerate(right_hops):
+                @pl.when(wanted)
+                def _():
+                    right_copy(left_piece(stream, piece), stream, hop, device, owned).start()
 
     def right_step(arriving):
         for stream in range(2):
@@ -164,19 +163,24 @@
                 def _():
                     right_copy(part, stream, hop, device, arriving).start()
 
-    right_start = jnp.where(row < 2, panel * pieces, (panel - PER_CLASS) * pieces)
+    longest = LAG * (n_x - 1)
+    right_start = jnp.where(
+        row < 2, panel * pieces + longest, (panel - PER_CLASS) * pieces + longest + 5
+    )
 
     def step(piece, carry):
-        @pl.when(piece < panel * pieces)
-        def _():
-            left_step(piece)
-
-        @pl.when(has_targets & jnp.logical_not(holder) & (piece >= right_start))
+        for stream in range(2):
+            lagged = piece - LAG * jnp.abs(x - stream)
+            @pl.when((lagged >= first_piece) & (lagged < panel * pieces))
+            def _():
+                left_step(stream, lagged)
+
+        @pl.when(has_targets & jnp.logical_not(holder) & (piece >= right_start) & (piece < right_start + PER_CLASS * pieces))
         def _():
             right_step(piece - right_start)
         return carry
 
-    lax.fori_loop(first_piece, right_start + PER_CLASS * pieces, step, 0)
+    lax.fori_loop(first_piece, jnp.maximum(right_start + PER_CLASS * pieces, panel * pieces + longest), step, 0)
 
     for copy in given:
         copy.wait()

time: 169 us -> 65 us (0.38)
  the two profiles are of different devices: /device:TPU:30 before, /device:TPU:29 now
where the time goes in v3:
time: 65 us; the launch traced here: 64.7 us
  Pallas kernels  58.4 us (90%)
  local copies, waits for them, and re-layouts  6.34 us (10%)
    pallas_call x1, Pallas kernels, per_device(): pl.pallas_call(functools.partial(kernel, n_row, n_col, n_x), out_shape=ja...  58.4 us
    unnamed x10, local copies, waits for them, and re-layouts  6.34 us

profile of v3, /device:TPU:29, one launch (start us, length us, event | category | flops | bytes accessed | tf_op | source)
XLA Modules:
  0.0 64.7 jit_solution(15098188851162833214)
XLA Ops:
  0.0 0.8 %copy.6.target_slots = s32[2,8,1]{2,1,0:T(8,128)S(1)} copy(s32[2,8,1]{1,2,0:T(1,128)} %param.7) | data formatting | bytes 128 | tf_op args[2]
  0.8 0.0 copy-start
  0.8 1.6 %copy-done = f32[8,1,256,256]{3,2,1,0:T(8,128)S(1)} copy-done((f32[8,1,256,256]{3,2,1,0:T(8,128)S(1)}, f32[8,1,256,256]{3,2,1,0:T(8,128)}, u32[]{:S(2)}) %copy-start) | copy-done | bytes 2097176
  2.4 0.0 copy-start.1
  2.4 1.0 %copy-done.1 = f32[2,256,256]{2,1,0:T(8,128)S(1)} copy-done((f32[2,256,256]{2,1,0:T(8,128)S(1)}, f32[2,256,256]{2,1,0:T(8,128)}, u32[]{:S(2)}) %copy-start.1) | copy-done | bytes 524312
  3.4 0.0 copy-start.2
  3.4 0.9 %copy-done.2 = f32[256,256]{1,0:T(8,128)S(1)} copy-done((f32[256,256]{1,0:T(8,128)S(1)}, f32[256,256]{1,0:T(8,128)}, u32[]{:S(2)}) %copy-start.2) | copy-done | bytes 262168
  4.3 0.0 copy-start.3
  4.3 0.7 %copy-done.3 = s32[2,4]{1,0:T(2,128)S(1)} copy-done((s32[2,4]{1,0:T(2,128)S(1)}, s32[2,4]{1,0:T(2,128)}, u32[]{:S(2)}) %copy-start.3) | copy-done | bytes 56
  5.0 58.4 %shard_map.55 = f32[8,1,256,256]{3,2,1,0:T(8,128)S(1)} custom-call(f32[8,1,256,256]{3,2,1,0:T(8,128)S(1)} %copy-done, s32[2,4]{1,0:T(2,128)S(1)} %copy-done.3, s32[2,8,1]{2,1,0:T(8,128)S(1)} %copy.6.target_slots, f32[2,256,256]{2,1,0:T(8,128)S(1)} %copy-done.1, f32[256,256]{1,0:T(8,128)S(1)} %copy-done.2), custom_call_target="tpu_custom_call" | custom-call | flops 3422552064 | bytes 4194304 | tf_op jit(solution)/shard_map/pallas_call | solution.py:301
  63.4 1.3 %copy.8 = f32[8,1,256,256]{3,2,1,0:T(8,128)} copy(f32[8,1,256,256]{3,2,1,0:T(8,128)S(1)} %shard_map.55) | data formatting | bytes 4194304
Async XLA Ops:
  0.8 1.6 %copy-start = (f32[8,1,256,256]{3,2,1,0:T(8,128)S(1)}, f32[8,1,256,256]{3,2,1,0:T(8,128)}, u32[]{:S(2)}) copy-start(f32[8,1,256,256]{3,2,1,0:T(8,128)} %blocks.1) | copy-start | bytes 6291460
  2.4 1.0 %copy-start.1 = (f32[2,256,256]{2,1,0:T(8,128)S(1)}, f32[2,256,256]{2,1,0:T(8,128)}, u32[]{:S(2)}) copy-start(f32[2,256,256]{2,1,0:T(8,128)} %inverse_in.1) | copy-start | bytes 1572868
  3.4 0.9 %copy-start.2 = (f32[256,256]{1,0:T(8,128)S(1)}, f32[256,256]{1,0:T(8,128)}, u32[]{:S(2)}) copy-start(f32[256,256]{1,0:T(8,128)} %cross_in.1) | copy-start | bytes 786436
  4.3 0.7 %copy-start.3 = (s32[2,4]{1,0:T(2,128)S(1)}, s32[2,4]{1,0:T(2,128)}, u32[]{:S(2)}) copy-start(s32[2,4]{1,0:T(2,128)} %panel_rows.1) | copy-start | bytes 100
